TPU v7x, 256 devices: a whole 4x4x8 slice. The times are simulated.
256 devices in a mesh: replica: 8 (over x_lo, y), fsdp: 32 (over z, x_hi, core).
Axes of the slice: x: 4 (x_hi: 2, x_lo: 2; x = x_hi * 2 + x_lo), y: 4, z: 8, core: 2. Of those that a mesh axis runs over, the one named last changes fastest.
Arguments:
- activations: bfloat16 [32768, 12288], P(('replica', 'fsdp')), may hold values from -24 to 24
- inner_weight: bfloat16 [8, 12288, 1024], P('replica', 'fsdp'), may hold values from -0.0546875 to 0.0546875
- out_cotangent: bfloat16 [32768, 1024], P(('replica', 'fsdp')), may hold values from -0.059814453 to 0.059814453
- local_fragment: bfloat16 [8, 512, 12288], P('replica', None, 'fsdp'), may hold values from -6 to 6
- outer_base: float32 [512, 12288], P('replica', 'fsdp'), may hold values from -6 to 6
- outer_momentum: float32 [512, 12288], P('replica', 'fsdp'), may hold values from -3 to 3
Outputs:
- inner_grad: float32 [8, 12288, 1024], P('replica', 'fsdp')
- new_base: float32 [512, 12288], P('replica', 'fsdp')
- new_momentum: float32 [512, 12288], P('replica', 'fsdp')
- merged_fragment: bfloat16 [8, 512, 12288], P('replica', None, 'fsdp')
All inputs are finite; a program needn't handle non-finite values.
Results may differ from a plain program's by a relative error of at most 0.012.
Values may be sent and summed in bfloat16 or wider, within the bound.
No kernel may reach another device: no remote copies, remote signals or barrier semaphores. Data moves between devices by JAX's collectives and lax.ppermute only.
A program may use at most 128 MiB of HBM per device.

v0:
```python
import jax
import jax.numpy as jnp
from jax import lax
from jax.sharding import PartitionSpec as P

HEAD = 128


def outer_update(base, momentum, total, count):
    delta = base - total / count
    momentum_next = 0.9 * momentum + delta
    base_next = base - 0.7 * (delta + 0.9 * momentum_next)
    return (base_next, momentum_next)


def norm_slope(pre, cotangent):
    heads = pre.reshape(pre.shape[0], pre.shape[1] // HEAD, HEAD)
    upstream = cotangent.astype(jnp.float32).reshape(heads.shape)
    inverse = lax.rsqrt(jnp.mean(heads * heads, axis=-1, keepdims=True) + 1e-06)
    normed = heads * inverse
    along = jnp.mean(upstream * normed, axis=-1, keepdims=True)
    return ((upstream - normed * along) * inverse).reshape(pre.shape).astype(jnp.bfloat16)


def body(activations, inner_weight, out_cotangent, local_fragment, outer_base, outer_momentum):
    weight = inner_weight[0]
    columns = activations
    pre = jnp.dot(
        columns,
        lax.all_gather(weight, "fsdp", axis=0, tiled=True),
        preferred_element_type=jnp.float32,
    )
    slope = norm_slope(pre, out_cotangent)
    columns = activations
    grad_local = lax.psum_scatter(
        lax.dot_general(
            columns, slope, (((0,), (0,)), ((), ())), preferred_element_type=jnp.float32
        ),
        "fsdp",
        scatter_dimension=0,
        tiled=True,
    )
    local_wide = local_fragment[0].astype(jnp.float32)
    count = lax.axis_size("replica")
    own_rows = outer_base.shape[0]
    total = lax.psum(local_wide.astype(jnp.bfloat16), "replica").astype(jnp.float32)
    base_full, moment_full = (
        lax.all_gather(outer_base, "replica", axis=0, tiled=True),
        lax.all_gather(outer_momentum, "replica", axis=0, tiled=True),
    )
    base_next, momentum_next = outer_update(base_full, moment_full, total, count)
    base_half = base_next.astype(jnp.bfloat16)
    offset = lax.axis_index("replica") * own_rows
    new_base = lax.dynamic_slice_in_dim(base_next, offset, own_rows, 0)
    new_momentum = lax.dynamic_slice_in_dim(momentum_next, offset, own_rows, 0)
    merged = (0.5 * base_half.astype(jnp.float32) + 0.5 * local_wide).astype(jnp.bfloat16)
    return (grad_local[None], new_base, new_momentum, merged[None])


def solution(mesh):
    placed = (
        P(("replica", "fsdp"), None),
        P("replica", "fsdp", None),
        P(("replica", "fsdp"), None),
        P("replica", None, "fsdp"),
        P("replica", "fsdp"),
        P("replica", "fsdp"),
    )
    return jax.shard_map(
        body,
        mesh=mesh,
        in_specs=placed,
        out_specs=(
            P("replica", "fsdp", None),
            P("replica", "fsdp"),
            P("replica", "fsdp"),
            P("replica", None, "fsdp"),
        ),
        check_vma=False,
    )
```

profile of v0, /device:TPU:2, one launch (start us, length us, event | category | flops | bytes accessed | tf_op | source)
XLA Modules:
  0.0 696.1 jit_solution(15459311280551665934)
XLA Ops:
  8.0 0.0 all-gather.3.cloned.1.call-start
  8.1 0.7 all-gather.3.cloned.1.call-update
  8.7 0.0 all-reduce.2.cloned.1.call-start
  8.8 0.5 all-reduce.2.cloned.1.call-update
  9.3 0.0 reduce-scatter.2.cloned.1.call-start
  9.4 1.0 convert_bitcast_fusion
  10.4 0.9 copy.13
  11.3 183.5 %all-gather.3.cloned.1.call-done = bf16[1,12288,1024]{2,1,0:T(8,128)(2,1)} async-done(((bf16[1,384,1024]{2,1,0:T(8,128)(2,1)}), bf16[1,12288,1024]{2,1,0:T(8,128)(2,1)}) %all-gather.3.cloned.1.call-update) | async-done | bytes 25165840 | tf_op jit(solution)/shard_map/all_gather | solution.py:30
  194.8 10.0 %fusion = f32[128,1024]{1,0:T(8,128)S(1)} fusion(bf16[128,12288]{1,0:T(8,128)(2,1)S(1)} %copy-done, bf16[1,12288,1024]{2,1,0:T(8,128)(2,1)} %all-gather.3.cloned.1.call-done), kind=kOutput, calls=%fused_computation.1 | convolution fusion | flops 3221225472 | bytes 28835840 | tf_op jit(solution)/shard_map/dot_general | solution.py:28
  204.9 0.8 copy-done.2
  205.7 0.1 copy.11
  205.8 0.2 multiply_reduce_fusion.1
  206.0 0.4 multiply_reduce_fusion
  206.4 1.0 mul.62
  207.4 1.0 mul.57
  208.4 20.9 %convolution_bitcast_fusion = f32[12288,1024]{0,1:T(8,128)} fusion(bf16[128,12288]{1,0:T(8,128)(2,1)S(1)} %copy-done, bf16[128,1024]{1,0:T(8,128)(2,1)S(1)} %copy-done.5, f32[16,8,8,128]{3,2,1,0:T(8,128)} %bitcast.33, f32[128,1024]{1,0:T(8,128)} %copy-done.2, f32[16,8,8,128]{3,2,1,0:T(8,128)} %bitcast.34), kind=kOutput, calls=%fused_computation | convolution fusion | flops 3222011904 | bytes 55312384 | tf_op jit(solution)/shard_map/dot_general | solution.py:36
  229.3 0.0 reduce-scatter.2.cloned.1.call-update
  229.3 0.9 copy-done.6
  230.2 31.8 %all_gather.10 = f32[512,384]{1,0:T(8,128)} all-gather(f32[64,384]{1,0:T(8,128)S(1)} %copy-done.6), channel_id=1, replica_groups=mesh['replica'=8,'fsdp'=32] {'replica'}, dimensions={0}, use_global_device_ids=true | all-gather | bytes 884736 | tf_op jit(solution)/shard_map/all_gather | solution.py:48
  262.0 31.9 %all_gather.11 = f32[512,384]{1,0:T(8,128)} all-gather(f32[64,384]{1,0:T(8,128)} %param.11), channel_id=1, replica_groups=mesh['replica'=8,'fsdp'=32] {'replica'}, dimensions={0}, use_global_device_ids=true | all-gather | bytes 884736 | tf_op jit(solution)/shard_map/all_gather | solution.py:49
  293.9 2.7 fusion.4
  296.6 0.7 constant_dynamic-slice_fusion
  297.3 388.4 %reduce-scatter.2.cloned.1.call-done = f32[384,1024]{0,1:T(8,128)} async-done(((f32[12288,1024]{0,1:T(8,128)}), f32[384,1024]{0,1:T(8,128)}) %reduce-scatter.2.cloned.1.call-update) | async-done | bytes 1572880 | tf_op jit(solution)/shard_map/reduce_scatter | solution.py:35
  685.6 3.0 copy.10
  (15 shorter events, 0.1 us)
Async XLA Ops:
  8.0 186.8 %copy-start = (bf16[128,12288]{1,0:T(8,128)(2,1)S(1)}, bf16[128,12288]{1,0:T(8,128)(2,1)}, u32[]{:S(2)}) copy-start(bf16[128,12288]{1,0:T(8,128)(2,1)} %param.6) | copy-start | bytes 9437188
  8.0 186.8 %all-gather.3.cloned.1.call-start = ((), (), s32[]{:S(2)}) async-start(), calls=%async_computation.3 | async-start | bytes 25952256 | tf_op jit(solution)/shard_map/all_gather | solution.py:30
  8.7 285.2 %all-reduce.2.cloned.1.call-start = ((), (), s32[]{:S(2)}) async-start(), calls=%async_computation.2 | async-start | bytes 786432 | tf_op jit(solution)/shard_map/psum | solution.py:46
  9.3 676.3 %reduce-scatter.2.cloned.1.call-start = ((), (), s32[]{:S(2)}) async-start(), calls=%async_computation.1 | async-start | bytes 51904512 | tf_op jit(solution)/shard_map/reduce_scatter | solution.py:35
  194.8 11.2 %copy-start.3 = (f32[16,8,8,128]{3,2,1,0:T(8,128)S(1)}, f32[16,8,8,128]{3,2,1,0:T(8,128)}, u32[]{:S(2)}) copy-start(f32[16,8,8,128]{3,2,1,0:T(8,128)} %copy.13) | copy-start | bytes 1572868
  204.9 0.8 copy-start.2
  204.9 3.6 copy-start.5
  229.3 0.9 copy-start.6
  229.3 64.6 %copy-start.4 = (bf16[1,512,384]{2,1,0:T(8,128)(2,1)S(1)}, bf16[1,512,384]{2,1,0:T(8,128)(2,1)}, u32[]{:S(2)}) copy-start(bf16[1,512,384]{2,1,0:T(8,128)(2,1)} %param.9) | copy-start | bytes 1179652
  262.0 426.7 %copy-start.1 = (bf16[128,12288]{1,0:T(8,128)(2,1)S(1)}, bf16[128,12288]{1,0:T(8,128)(2,1)}, u32[]{:S(2)}) copy-start(bf16[128,12288]{1,0:T(8,128)(2,1)} %param.6) | copy-start | bytes 9437188
Sparse Core Ops, SparseCore 0:
  11.6 183.1 all-gather.2
  229.4 456.1 reduce-scatter.1
Sparse Core Ops, SparseCore 1:
  12.0 153.9 all-reduce.1
where the time goes:
time: 698 us; the launch traced here: 696 us
  waiting for transfers between devices  573 us (82%)
  blocking collectives  63.8 us (9%)
  matrix products  30.9 us (4%)
  between operations  15.6 us (2%)
  local copies, waits for them, and re-layouts  8.38 us (1%)
    reduce_scatter x1, waiting for transfers between devices, body(): lax.psum_scatter(lax.dot_general(columns, slope, (((0,), (0,)), ((), ()))...  388 us
    all_gather x1, waiting for transfers between devices, body(): lax.all_gather(weight, 'fsdp', axis=0, tiled=True)  184 us
    all_gather x1, blocking collectives, body(): lax.all_gather(outer_momentum, 'replica', axis=0, tiled=True)  31.9 us
    all_gather x1, blocking collectives, body(): lax.all_gather(outer_base, 'replica', axis=0, tiled=True)  31.8 us
    dot_general x1, matrix products, body(): lax.dot_general(columns, slope, (((0,), (0,)), ((), ())), preferred_eleme...  20.9 us
  transfers between devices with their start and end apart: 3, of which 2 were waited for; matrix products, arithmetic and copies ran while one was open for 6% of the time, Pallas kernels for 0%

commit v1 on v0

v1 whole, which is shorter than its diff:
```python
import jax
import jax.numpy as jnp
from jax import lax
from jax.experimental import pallas as pl
from jax.experimental.pallas import tpu as pltpu
from jax.sharding import Mesh, PartitionSpec as P

HEAD = 128
CUTS = 2
F32, BF16 = jnp.float32, jnp.bfloat16
RIGHT = [(i, (i + 1) % 8) for i in range(8)]
LEFT = [(i, (i + 7) % 8) for i in range(8)]
SWAP = [(0, 1), (1, 0)]
BOTH = [(0, 3), (1, 2), (2, 1), (3, 0)]
FAR = [(0, 2), (1, 3), (2, 0), (3, 1)]
NEAR = [(0, 1), (1, 0), (2, 3), (3, 2)]


VMEM = pl.BlockSpec(memory_space=pltpu.VMEM)
SMEM = pl.BlockSpec(memory_space=pltpu.SMEM)
ROOM = pltpu.CompilerParams(vmem_limit_bytes=16 << 20)


def slopes_of(own, from_core, from_x, cotangent):
    tokens, width = own.shape

    def kernel(own_ref, core_ref, x_ref, cot_ref, out_ref):
        for h in range(width // HEAD):
            at = slice(h * HEAD, (h + 1) * HEAD)
            heads = own_ref[:, at] + core_ref[0, :, at].astype(F32) + x_ref[:, at].astype(F32)
            upstream = cot_ref[:, at].astype(F32)
            inverse = lax.rsqrt(jnp.mean(heads * heads, axis=-1, keepdims=True) + 1e-06)
            normed = heads * inverse
            along = jnp.mean(upstream * normed, axis=-1, keepdims=True)
            out_ref[:, at] = ((upstream - normed * along) * inverse).astype(BF16)

    return pl.pallas_call(
        kernel,
        in_specs=[VMEM] * 4,
        out_specs=VMEM,
        out_shape=jax.ShapeDtypeStruct((tokens, width), BF16),
        compiler_params=ROOM,
    )(own, from_core, from_x, cotangent)


def project(pieces, found):
    tokens, rows = pieces[0].shape[1:]
    width = found[0][1].shape[-1]

    def kernel(*refs):
        held, weights, total, blocks = refs[:4], refs[4 : 4 + len(found)], refs[4 + len(found)], refs[5 + len(found) :]
        for d in range(8):
            for k in range(4):
                blocks[d][k * tokens : (k + 1) * tokens, :] = held[k][d]
        for i, ((d, _), weight) in enumerate(zip(found, weights)):
            term = jnp.dot(blocks[d % 8][...], weight[...], preferred_element_type=F32)
            if i:
                total[...] += term
            else:
                total[...] = term

    total, *blocks = pl.pallas_call(
        kernel,
        in_specs=[VMEM] * (4 + len(found)),
        out_specs=[VMEM] * 9,
        out_shape=[jax.ShapeDtypeStruct((4 * tokens, width), F32)]
        + [jax.ShapeDtypeStruct((4 * tokens, rows), BF16)] * 8,
        compiler_params=ROOM,
    )(*pieces, *(block for _, block in found))
    return total, blocks


def complete(total, block, ends):
    tokens, width = total.shape[0] // 4, total.shape[1] // CUTS
    half = ends[0].shape[0]

    def kernel(total_ref, block_ref, up_ref, down_ref, *outs):
        for i in range(CUTS):
            at = slice(i * width, (i + 1) * width)
            sums = (
                total_ref[:, at]
                + jnp.dot(block_ref[:, :half], up_ref[:, at], preferred_element_type=F32)
                + jnp.dot(block_ref[:, half:], down_ref[:, at], preferred_element_type=F32)
            )
            own, over_x, crossing = outs[3 * i : 3 * i + 3]
            own[...] = sums[:tokens]
            over_x[...] = sums[tokens : 2 * tokens]
            crossing[0] = sums[2 * tokens : 3 * tokens].astype(BF16)
            crossing[1] = sums[3 * tokens :].astype(BF16)

    outs = pl.pallas_call(
        kernel,
        in_specs=[VMEM] * 4,
        out_specs=[VMEM] * (3 * CUTS),
        out_shape=[
            jax.ShapeDtypeStruct((tokens, width), F32),
            jax.ShapeDtypeStruct((tokens, width), F32),
            jax.ShapeDtypeStruct((2, tokens, width), BF16),
        ]
        * CUTS,
        compiler_params=ROOM,
    )(total, block, *ends)
    return [outs[3 * i : 3 * i + 3] for i in range(CUTS)]


def split_columns(rows, mine, z):
    tokens, width = rows.shape[0], rows.shape[1] // 32
    holds = ((2, 0, 8), (3, 0, 8), (1, 0, 8), (0, 0, 8))

    def kernel(mine_ref, z_ref, rows_ref, *refs):
        copies = []
        for (k, begin, count), out in zip(holds, refs):
            member = mine_ref[0] ^ k
            for i in range(count):
                at = lax.rem(z_ref[0] + begin + i, 8)
                start = pl.multiple_of((4 * at + member) * width, width)
                copies.append(
                    pltpu.make_async_copy(
                        rows_ref.at[:, pl.ds(start, width)], out.at[i], refs[-1].at[k, begin + i]
                    )
                )
                copies[-1].start()
        for copy in copies:
            copy.wait()

    over_x, over_both, core, own = pl.pallas_call(
        kernel,
        in_specs=[SMEM, SMEM, pl.BlockSpec(memory_space=pl.ANY)],
        out_specs=[VMEM] * len(holds),
        out_shape=[jax.ShapeDtypeStruct((count, tokens, width), rows.dtype) for _, _, count in holds],
        scratch_shapes=[pltpu.SemaphoreType.DMA((4, 8))],
        compiler_params=pltpu.CompilerParams(vmem_limit_bytes=16 << 20),
    )(mine, z, rows)
    return own, core, over_x, over_both


def tie(value, *others):
    return lax.optimization_barrier((value, *others))[0]


def step(pair, *others):
    pair = lax.optimization_barrier((*pair, *others))
    return lax.ppermute(pair[0], "z", RIGHT), lax.ppermute(pair[1], "z", LEFT)


def ends(pair):
    half = pair[0].shape[0] // 2
    return pair[0][:half], pair[1][half:]


def plus(part, arrived):
    return (part + arrived.astype(F32)).astype(BF16)


def beside(part_of, arrived):
    up, down = arrived
    half = up.shape[0]
    ahead, behind = part_of(3), part_of(-3)
    return (
        jnp.concatenate([plus(ahead[:half], up), ahead[half:].astype(BF16)]),
        jnp.concatenate([behind[:half].astype(BF16), plus(behind[half:], down)]),
    )


def onward(part_of, arrived, d):
    return plus(part_of(d), arrived[0]), plus(part_of(-d), arrived[1])


def home(part_of, arrived):
    return part_of(0) + arrived[0].astype(F32) + arrived[1].astype(F32)


def body(activations, inner_weight, out_cotangent, local_fragment, outer_base, outer_momentum):
    weight, fragment = inner_weight[0], local_fragment[0]
    y = lax.axis_index("y")
    mine = lax.axis_index("xh") * 2 + lax.axis_index("c")
    bits = [(y & 2) == 2, (y & 1) == 1, lax.axis_index("xl") == 1]
    weight, activations, fragment, z, mine, *bits = lax.optimization_barrier(
        (weight, activations, fragment, lax.axis_index("z").reshape(1), mine.reshape(1), *bits)
    )

    own_rows, own_columns = outer_base.shape
    stages = ((1, "y", FAR), (2, "y", NEAR), (0, "xl", SWAP))

    def halve(total, stage, *others):
        at, axis, moves = stages[stage]
        low, high = jnp.split(total, 2, axis=at)
        sent = tie(jnp.where(bits[stage], low, high), *others)
        return jnp.where(bits[stage], high, low).astype(F32) + lax.ppermute(sent, axis, moves).astype(F32)

    def double(rows, stage, *others):
        at, axis, moves = stages[stage]
        other = lax.ppermute(tie(rows, *others), axis, moves)
        low, high = jnp.where(bits[stage], other, rows), jnp.where(bits[stage], rows, other)
        return jnp.concatenate([low, high], axis=at)

    a1 = step((weight, weight))
    own, core, over_x, over_both = split_columns(activations, mine, z)
    from_x = lax.ppermute(over_x, "xh", SWAP)
    from_core = lax.ppermute(core, "c", SWAP)
    a2 = step(a1)
    from_both = lax.ppermute(tie(over_both, from_x), ("xh", "c"), BOTH)
    total = halve(fragment.reshape(2, 2, 2, own_rows, own_columns), 0, *a1)
    a3 = step(a2, from_core, total)
    total = halve(total, 1, *a2)
    a4 = step(ends(a3), total)

    found = [(0, weight)]
    for d, pair in enumerate((a1, a2, a3), 1):
        found += [(-d, pair[0]), (d, pair[1])]
    sums, blocks = project((own, from_x, from_core, from_both), found)
    total = halve(total, 2, sums)
    partial = complete(sums, blocks[4], a4)
    width = weight.shape[1] // CUTS

    def part_with(slopes):
        return lambda d: lax.dot_general(
            blocks[d % 8], slopes, (((0,), (0,)), ((), ())), preferred_element_type=F32
        )

    def slopes_from(own, from_core, from_x, cut):
        cotangent = out_cotangent[:, cut * width : (cut + 1) * width]
        mine = slopes_of(own, from_core, from_x, cotangent)
        pair = jnp.stack([mine, lax.ppermute(mine, "xh", SWAP)])
        return jnp.concatenate([pair, lax.ppermute(pair, "c", SWAP)]).reshape(-1, width)

    crossed = [lax.ppermute(crossing, "c", SWAP) for _, _, crossing in partial]
    arrived = [
        lax.ppermute(plus(over_x, from_core[1]), "xh", SWAP)
        for (_, over_x, _), from_core in zip(partial, crossed)
    ]
    slopes = slopes_from(partial[0][0], crossed[0], arrived[0], 0)
    first = part_with(slopes)

    far = first(4).astype(BF16)
    t1 = step(ends((far, far)), arrived[1])
    slopes = slopes_from(partial[1][0], crossed[1], arrived[1], 1)
    second = part_with(slopes)
    delta = outer_base - total.reshape(own_rows, own_columns) / 8
    new_momentum = 0.9 * outer_momentum + delta
    new_base = outer_base - 0.7 * (delta + 0.9 * new_momentum)
    half_base = double(new_base.astype(BF16).reshape(1, 1, 1, own_rows, own_columns), 2)
    t2 = step(beside(first, t1), half_base)
    half_base = double(half_base, 1, *t1)
    far = second(4).astype(BF16)
    t3 = step(onward(first, t2, 2), slopes, half_base)
    u1 = step(ends((far, far)), *t2)
    half_base = double(half_base, 0, *t2)
    t4 = step(onward(first, t3, 1), *u1, half_base)
    u2 = step(beside(second, u1), *t3)
    u3 = step(onward(second, u2, 2), *t4)
    u4 = step(onward(second, u3, 1))
    grad = jnp.concatenate([home(first, t4), home(second, u4)], axis=1)
    half_base = half_base.reshape(fragment.shape)
    merged = (0.5 * half_base.astype(F32) + 0.5 * fragment.astype(F32)).astype(BF16)
    return grad[None], new_base, new_momentum, merged[None]


def solution(mesh):
    axes = ("xl", "y", "z", "xh", "c")
    mesh = Mesh(mesh.devices.reshape(2, 4, 8, 2, 2), axes)
    replica, fsdp = ("xl", "y"), ("z", "xh", "c")
    placed = (
        P(axes, None),
        P(replica, fsdp, None),
        P(axes, None),
        P(replica, None, fsdp),
        P(replica, fsdp),
        P(replica, fsdp),
    )
    return jax.shard_map(
        body,
        mesh=mesh,
        in_specs=placed,
        out_specs=(
            P(replica, fsdp, None),
            P(replica, fsdp),
            P(replica, fsdp),
            P(replica, None, fsdp),
        ),
        check_vma=False,
    )
```

time: 698 us -> 193 us (0.28)
  waiting for transfers between devices: 573 us -> 101 us
  starting transfers between devices: 0.12 us -> 70.3 us
  blocking collectives: 63.8 us -> 0 us
  matrix products: 30.9 us -> 6.31 us
  between operations: 15.6 us -> 1.34 us
    reduce_scatter x1 -> x0, waiting for transfers between devices: 388 us -> none  [body(): lax.psum_scatter(lax.dot_general(columns, slope, (((0,), (0,)), ((), ()))...]
    all_gather x1 -> x0, waiting for transfers between devices: 184 us -> none  [body(): lax.all_gather(weight, 'fsdp', axis=0, tiled=True)]
    ppermute x0 -> x41, waiting for transfers between devices: none -> 101 us  [the longest x24 80.8 us: step(): return (lax.ppermute(pair[0], 'z', RIGHT), lax.ppermute(pair[1], 'z', LEFT))]
    ppermute x0 -> x41, starting transfers between devices: none -> 70.3 us  [the longest x24 39.7 us: step(): return (lax.ppermute(pair[0], 'z', RIGHT), lax.ppermute(pair[1], 'z', LEFT))]
    all_gather x2 -> x0, blocking collectives: 63.8 us -> none  [the longest x1 31.9 us: body(): lax.all_gather(outer_momentum, 'replica', axis=0, tiled=True)]
    dot_general x2 -> x16, matrix products: 30.9 us -> 6.31 us  [part_with(): lax.dot_general(blocks[d % 8], slopes, (((0,), (0,)), ((), ())), preferre...]
  transfers between devices with their start and end apart: 3 -> 41, of which waited for: 2 -> 23; matrix products, arithmetic and copies ran while one was open for 6% -> 4% of each run, Pallas kernels for 0% -> 3%
where the time goes in v1:
time: 193 us; the launch traced here: 191 us
  waiting for transfers between devices  101 us (52%)
  starting transfers between devices  70.3 us (36%)
  matrix products  6.31 us (3%)
  Pallas kernels  6.2 us (3%)
  other arithmetic  3.76 us (2%)
  local copies, waits for them, and re-layouts  2.24 us (1%)
    ppermute x24, waiting for transfers between devices, step(): return (lax.ppermute(pair[0], 'z', RIGHT), lax.ppermute(pair[1], 'z', LEFT))  80.8 us
    ppermute x24, starting transfers between devices, step(): return (lax.ppermute(pair[0], 'z', RIGHT), lax.ppermute(pair[1], 'z', LEFT))  39.7 us
    ppermute x3, starting transfers between devices, double(): other = lax.ppermute(tie(rows, *others), axis, moves)  14.5 us
    ppermute x3, starting transfers between devices, halve(): lax.ppermute(sent, axis, moves).astype(F32)  6.32 us
    dot_general x16, matrix products, part_with(): lax.dot_general(blocks[d % 8], slopes, (((0,), (0,)), ((), ())), preferre...  6.31 us
    ppermute x2, waiting for transfers between devices, slopes_from(): pair = jnp.stack([mine, lax.ppermute(mine, 'xh', SWAP)])  5.34 us
    ppermute x3, waiting for transfers between devices, halve(): lax.ppermute(sent, axis, moves).astype(F32)  4.87 us
    ppermute x2, waiting for transfers between devices, body(): lax.ppermute(plus(over_x, from_core[1]), 'xh', SWAP)  4.24 us
  transfers between devices with their start and end apart: 41, of which 23 were waited for; matrix products, arithmetic and copies ran while one was open for 4% of the time, Pallas kernels for 3%

profile of v1, /device:TPU:2, one launch (start us, length us, event | category | flops | bytes accessed | tf_op | source)
XLA Modules:
  0.0 190.8 jit_solution(14397864231734327845)
XLA Ops:
  2.6 4.0 %collective-permute-start.4 = (bf16[384,1024]{1,0:T(8,128)(2,1)}, bf16[384,1024]{1,0:T(8,128)(2,1)S(1)}, u32[]{:S(2)}, u32[]{:S(2)}) collective-permute-start(bf16[384,1024]{1,0:T(8,128)(2,1)} %bitcast.71), channel_id=1, source_target_pairs={{0,28},{4,0},{8,4},{12,8},{16,12},{20,16},{24,20},{28,24},{1,29},{... | collective-permute-start | bytes 2359304 | tf_op jit(solution)/shard_map/ppermute | solution.py:143
  9.7 14.6 %collective-permute-done.3.refs_5_ = bf16[384,1024]{1,0:T(8,128)(2,1)S(1)} collective-permute-done((bf16[384,1024]{1,0:T(8,128)(2,1)}, bf16[384,1024]{1,0:T(8,128)(2,1)S(1)}, u32[]{:S(2)}, u32[]{:S(2)}) %collective-permute-start.3) | collective-permute-done | bytes 786464 | tf_op jit(solution)/shard_map/ppermute | solution.py:143
  24.3 3.2 %collective-permute-start.6 = (bf16[384,1024]{1,0:T(8,128)(2,1)S(1)}, bf16[384,1024]{1,0:T(8,128)(2,1)S(1)}, u32[]{:S(2)}, u32[]{:S(2)}) collective-permute-start(bf16[384,1024]{1,0:T(8,128)(2,1)S(1)} %collective-permute-done.4.refs_6_), channel_id=1, source_target_pairs={{0,28},{4,0},{8,4},{12,8},{16,12},{20,16},{24,20},{28,24},{1,29},{... | collective-permute-start | bytes 2359304 | tf_op jit(solution)/shard_map/ppermute | solution.py:143
  27.6 3.3 %collective-permute-start.7 = (bf16[2,1,2,64,384]{4,3,2,1,0:T(8,128)(2,1)S(1)}, bf16[2,1,2,64,384]{4,3,2,1,0:T(8,128)(2,1)S(1)}, u32[]{:S(2)}, u32[]{:S(2)}) collective-permute-start(bf16[2,1,2,64,384]{4,3,2,1,0:T(8,128)(2,1)S(1)} %broadcast_select_fusion.2), channel_id=1, source_target_pairs={{0,64},{32,96},{64,0},{96,32},{1,65},{33,97},{65,1},{97,33},{2,66}... | collective-permute-start | bytes 589832 | tf_op jit(solution)/shard_map/ppermute | solution.py:189
  35.0 9.3 %collective-permute-done.5.refs_7_ = bf16[384,1024]{1,0:T(8,128)(2,1)S(1)} collective-permute-done((bf16[384,1024]{1,0:T(8,128)(2,1)S(1)}, bf16[384,1024]{1,0:T(8,128)(2,1)S(1)}, u32[]{:S(2)}, u32[]{:S(2)}) %collective-permute-start.5) | collective-permute-done | bytes 786464 | tf_op jit(solution)/shard_map/ppermute | solution.py:143
  50.3 3.0 %collective-permute-done.10 = f32[2,1,1,64,384]{4,3,2,1,0:T(8,128)S(1)} collective-permute-done((f32[2,1,1,64,384]{4,3,2,1,0:T(8,128)S(1)}, f32[2,1,1,64,384]{4,3,2,1,0:T(8,128)S(1)}, u32[]{:S(2)}, u32[]{:S(2)}) %collective-permute-start.10) | collective-permute-done | bytes 196640 | tf_op jit(solution)/shard_map/ppermute | solution.py:189
  53.3 10.0 %collective-permute-done.8.refs_9_ = bf16[384,1024]{1,0:T(8,128)(2,1)S(1)} collective-permute-done((bf16[384,1024]{1,0:T(8,128)(2,1)S(1)}, bf16[384,1024]{1,0:T(8,128)(2,1)S(1)}, u32[]{:S(2)}, u32[]{:S(2)}) %collective-permute-start.8) | collective-permute-done | bytes 786464 | tf_op jit(solution)/shard_map/ppermute | solution.py:143
  66.9 3.9 %collective-permute-done.2.refs_3_ = bf16[8,128,384]{2,1,0:T(8,128)(2,1)S(1)} collective-permute-done((bf16[8,128,384]{2,1,0:T(8,128)(2,1)S(1)}, bf16[8,128,384]{2,1,0:T(8,128)(2,1)S(1)}, u32[]{:S(2)}, u32[]{:S(2)}) %collective-permute-start.2) | collective-permute-done | bytes 786464 | tf_op jit(solution)/shard_map/ppermute | solution.py:202
  70.8 3.9 %shard_map.94 = (f32[512,1024]{1,0:T(8,128)S(1)}, bf16[512,384]{1,0:T(8,128)(2,1)S(1)}, bf16[512,384]{1,0:T(8,128)(2,1)S(1)}, bf16[512,384]{1,0:T(8,128)(2,1)S(1...) custom-call(bf16[8,128,384]{2,1,0:T(8,128)(2,1)S(1)} %get-tuple-elem, ...), custom_call_target="tpu_custom_call" | custom-call | tf_op jit(solution)/shard_map/pallas_call | solution.py:62
  81.4 4.2 %collective-permute-done.14.x_ref = bf16[128,512]{1,0:T(8,128)(2,1)S(1)} collective-permute-done((bf16[128,512]{1,0:T(8,128)(2,1)S(1)}, bf16[128,512]{1,0:T(8,128)(2,1)S(1)}, u32[]{:S(2)}, u32[]{:S(2)}) %collective-permute-start.14) | collective-permute-done | bytes 131104 | tf_op jit(solution)/shard_map/ppermute | solution.py:229
  93.5 2.8 %collective-permute-done.25 = bf16[128,512]{1,0:T(8,128)(2,1)S(1)} collective-permute-done((bf16[128,512]{1,0:T(8,128)(2,1)S(1)}, bf16[128,512]{1,0:T(8,128)(2,1)S(1)}, u32[]{:S(2)}, u32[]{:S(2)}) %collective-permute-start.25) | collective-permute-done | bytes 131104 | tf_op jit(solution)/shard_map/ppermute | solution.py:224
  102.6 4.6 %collective-permute-done.19 = bf16[192,512]{1,0:T(8,128)(2,1)S(1)} collective-permute-done((bf16[192,512]{1,0:T(8,128)(2,1)S(1)}, bf16[192,512]{1,0:T(8,128)(2,1)S(1)}, u32[]{:S(2)}, u32[]{:S(2)}) %collective-permute-start.19) | collective-permute-done | bytes 196640 | tf_op jit(solution)/shard_map/ppermute | solution.py:143
  107.1 10.8 %collective-permute-start.27 = (bf16[2,1,1,64,384]{4,3,2,1,0:T(8,128)(2,1)S(1)}, bf16[2,1,1,64,384]{4,3,2,1,0:T(8,128)(2,1)S(1)}, u32[]{:S(2)}, u32[]{:S(2)}) collective-permute-start(bf16[2,1,1,64,384]{4,3,2,1,0:T(8,128)(2,1)S(1)} %pad_maximum_fusion.10), channel_id=1, source_target_pairs={{0,32},{32,0},{64,96},{96,64},{1,33},{33,1},{65,97},{97,65},{2,34}... | collective-permute-start | bytes 294920 | tf_op jit(solution)/shard_map/ppermute | solution.py:193
  121.7 8.1 %collective-permute-done.23 = bf16[384,512]{1,0:T(8,128)(2,1)S(1)} collective-permute-done((bf16[384,512]{1,0:T(8,128)(2,1)S(1)}, bf16[384,512]{1,0:T(8,128)(2,1)S(1)}, u32[]{:S(2)}, u32[]{:S(2)}) %collective-permute-start.23) | collective-permute-done | bytes 393248 | tf_op jit(solution)/shard_map/ppermute | solution.py:143
  129.8 2.9 %collective-permute-start.32 = (bf16[2,1,2,64,384]{4,3,2,1,0:T(8,128)(2,1)S(1)}, bf16[2,1,2,64,384]{4,3,2,1,0:T(8,128)(2,1)S(1)}, u32[]{:S(2)}, u32[]{:S(2)}) collective-permute-start(bf16[2,1,2,64,384]{4,3,2,1,0:T(8,128)(2,1)S(1)} %pad_maximum_fusion.9), channel_id=1, source_target_pairs={{0,64},{32,96},{64,0},{96,32},{1,65},{33,97},{65,1},{97,33},{2,66}... | collective-permute-start | bytes 589832 | tf_op jit(solution)/shard_map/ppermute | solution.py:193
  133.5 3.0 %collective-permute-start.29 = (bf16[384,512]{1,0:T(8,128)(2,1)S(1)}, bf16[384,512]{1,0:T(8,128)(2,1)S(1)}, u32[]{:S(2)}, u32[]{:S(2)}) collective-permute-start(bf16[384,512]{1,0:T(8,128)(2,1)S(1)} %fusion.4), channel_id=1, source_target_pairs={{0,28},{4,0},{8,4},{12,8},{16,12},{20,16},{24,20},{28,24},{1,29},{... | collective-permute-start | bytes 1179656 | tf_op jit(solution)/shard_map/ppermute | solution.py:143
  137.0 2.9 %collective-permute-start.31 = (bf16[192,512]{1,0:T(8,128)(2,1)S(1)}, bf16[192,512]{1,0:T(8,128)(2,1)S(1)}, u32[]{:S(2)}, u32[]{:S(2)}) collective-permute-start(bf16[192,512]{1,0:T(8,128)(2,1)S(1)} %get-tuple-element.108), channel_id=1, source_target_pairs={{0,28},{4,0},{8,4},{12,8},{16,12},{20,16},{24,20},{28,24},{1,29},{... | collective-permute-start | bytes 589832 | tf_op jit(solution)/shard_map/ppermute | solution.py:143
  139.9 7.4 %collective-permute-done.31 = bf16[192,512]{1,0:T(8,128)(2,1)S(1)} collective-permute-done((bf16[192,512]{1,0:T(8,128)(2,1)S(1)}, bf16[192,512]{1,0:T(8,128)(2,1)S(1)}, u32[]{:S(2)}, u32[]{:S(2)}) %collective-permute-start.31) | collective-permute-done | bytes 196640 | tf_op jit(solution)/shard_map/ppermute | solution.py:143
  147.4 3.3 %collective-permute-done.30 = bf16[192,512]{1,0:T(8,128)(2,1)S(1)} collective-permute-done((bf16[192,512]{1,0:T(8,128)(2,1)S(1)}, bf16[192,512]{1,0:T(8,128)(2,1)S(1)}, u32[]{:S(2)}, u32[]{:S(2)}) %collective-permute-start.30) | collective-permute-done | bytes 196640 | tf_op jit(solution)/shard_map/ppermute | solution.py:143
  153.8 3.2 %collective-permute-start.34 = (bf16[384,512]{1,0:T(8,128)(2,1)S(1)}, bf16[384,512]{1,0:T(8,128)(2,1)S(1)}, u32[]{:S(2)}, u32[]{:S(2)}) collective-permute-start(bf16[384,512]{1,0:T(8,128)(2,1)S(1)} %fusion.5), channel_id=1, source_target_pairs={{0,28},{4,0},{8,4},{12,8},{16,12},{20,16},{24,20},{28,24},{1,29},{... | collective-permute-start | bytes 1179656 | tf_op jit(solution)/shard_map/ppermute | solution.py:143
  157.0 5.8 %collective-permute-done.36 = bf16[384,512]{1,0:T(8,128)(2,1)S(1)} collective-permute-done((bf16[384,512]{1,0:T(8,128)(2,1)S(1)}, bf16[384,512]{1,0:T(8,128)(2,1)S(1)}, u32[]{:S(2)}, u32[]{:S(2)}) %collective-permute-start.36) | collective-permute-done | bytes 393248 | tf_op jit(solution)/shard_map/ppermute | solution.py:143
  164.8 3.8 %collective-permute-done.33 = bf16[384,512]{1,0:T(8,128)(2,1)S(1)} collective-permute-done((bf16[384,512]{1,0:T(8,128)(2,1)S(1)}, bf16[384,512]{1,0:T(8,128)(2,1)S(1)}, u32[]{:S(2)}, u32[]{:S(2)}) %collective-permute-start.33) | collective-permute-done | bytes 393248 | tf_op jit(solution)/shard_map/ppermute | solution.py:143
  170.7 6.2 %collective-permute-done.38 = bf16[384,512]{1,0:T(8,128)(2,1)S(1)} collective-permute-done((bf16[384,512]{1,0:T(8,128)(2,1)S(1)}, bf16[384,512]{1,0:T(8,128)(2,1)S(1)}, u32[]{:S(2)}, u32[]{:S(2)}) %collective-permute-start.38) | collective-permute-done | bytes 393248 | tf_op jit(solution)/shard_map/ppermute | solution.py:143
  183.8 4.4 %collective-permute-done.39 = bf16[384,512]{1,0:T(8,128)(2,1)S(1)} collective-permute-done((bf16[384,512]{1,0:T(8,128)(2,1)S(1)}, bf16[384,512]{1,0:T(8,128)(2,1)S(1)}, u32[]{:S(2)}, u32[]{:S(2)}) %collective-permute-start.39) | collective-permute-done | bytes 393248 | tf_op jit(solution)/shard_map/ppermute | solution.py:143
  (128 shorter events, 60.8 us)
Async XLA Ops:
  0.6 23.7 %collective-permute-start.3 = (bf16[384,1024]{1,0:T(8,128)(2,1)}, bf16[384,1024]{1,0:T(8,128)(2,1)S(1)}, u32[]{:S(2)}, u32[]{:S(2)}) collective-permute-start(bf16[384,1024]{1,0:T(8,128)(2,1)} %bitcast.70), channel_id=1, source_target_pairs={{0,4},{4,8},{8,12},{12,16},{16,20},{20,24},{24,28},{28,0},{1,5},{5... | collective-permute-start | bytes 2359304 | tf_op jit(solution)/shard_map/ppermute | solution.py:143
  2.6 21.7 %collective-permute-start.4 = (bf16[384,1024]{1,0:T(8,128)(2,1)}, bf16[384,1024]{1,0:T(8,128)(2,1)S(1)}, u32[]{:S(2)}, u32[]{:S(2)}) collective-permute-start(bf16[384,1024]{1,0:T(8,128)(2,1)} %bitcast.71), channel_id=1, source_target_pairs={{0,28},{4,0},{8,4},{12,8},{16,12},{20,16},{24,20},{28,24},{1,29},{... | collective-permute-start | bytes 2359304 | tf_op jit(solution)/shard_map/ppermute | solution.py:143
  9.6 25.3 %collective-permute-start.1 = (bf16[8,128,384]{2,1,0:T(8,128)(2,1)S(1)}, bf16[8,128,384]{2,1,0:T(8,128)(2,1)S(1)}, u32[]{:S(2)}, u32[]{:S(2)}) collective-permute-start(bf16[8,128,384]{2,1,0:T(8,128)(2,1)S(1)} %get-tuple-element.66), channel_id=1, source_target_pairs={{0,1},{1,0},{2,3},{3,2},{4,5},{5,4},{6,7},{7,6},{8,9},{9,8},{10,11... | collective-permute-start | bytes 2359304 | tf_op jit(solution)/shard_map/ppermute | solution.py:200
  24.3 19.9 %collective-permute-start.5 = (bf16[384,1024]{1,0:T(8,128)(2,1)S(1)}, bf16[384,1024]{1,0:T(8,128)(2,1)S(1)}, u32[]{:S(2)}, u32[]{:S(2)}) collective-permute-start(bf16[384,1024]{1,0:T(8,128)(2,1)S(1)} %collective-permute-done.3.refs_5_), channel_id=1, source_target_pairs={{0,4},{4,8},{8,12},{12,16},{16,20},{20,24},{24,28},{28,0},{1,5},{5... | collective-permute-start | bytes 2359304 | tf_op jit(solution)/shard_map/ppermute | solution.py:143
  24.3 19.9 %collective-permute-start.6 = (bf16[384,1024]{1,0:T(8,128)(2,1)S(1)}, bf16[384,1024]{1,0:T(8,128)(2,1)S(1)}, u32[]{:S(2)}, u32[]{:S(2)}) collective-permute-start(bf16[384,1024]{1,0:T(8,128)(2,1)S(1)} %collective-permute-done.4.refs_6_), channel_id=1, source_target_pairs={{0,28},{4,0},{8,4},{12,8},{16,12},{20,16},{24,20},{28,24},{1,29},{... | collective-permute-start | bytes 2359304 | tf_op jit(solution)/shard_map/ppermute | solution.py:143
  30.9 19.4 %collective-permute-start = (bf16[8,128,384]{2,1,0:T(8,128)(2,1)S(1)}, bf16[8,128,384]{2,1,0:T(8,128)(2,1)S(1)}, u32[]{:S(2)}, u32[]{:S(2)}) collective-permute-start(bf16[8,128,384]{2,1,0:T(8,128)(2,1)S(1)} %get-tuple-element.65), channel_id=1, source_target_pairs={{0,2},{2,0},{1,3},{3,1},{4,6},{6,4},{5,7},{7,5},{8,10},{10,8},{9,1... | collective-permute-start | bytes 2359304 | tf_op jit(solution)/shard_map/ppermute | solution.py:199
  44.3 19.0 %collective-permute-start.8 = (bf16[384,1024]{1,0:T(8,128)(2,1)S(1)}, bf16[384,1024]{1,0:T(8,128)(2,1)S(1)}, u32[]{:S(2)}, u32[]{:S(2)}) collective-permute-start(bf16[384,1024]{1,0:T(8,128)(2,1)S(1)} %collective-permute-done.5.refs_7_), channel_id=1, source_target_pairs={{0,4},{4,8},{8,12},{12,16},{16,20},{20,24},{24,28},{28,0},{1,5},{5... | collective-permute-start | bytes 2359304 | tf_op jit(solution)/shard_map/ppermute | solution.py:143
  46.1 17.2 %collective-permute-start.9 = (bf16[384,1024]{1,0:T(8,128)(2,1)S(1)}, bf16[384,1024]{1,0:T(8,128)(2,1)S(1)}, u32[]{:S(2)}, u32[]{:S(2)}) collective-permute-start(bf16[384,1024]{1,0:T(8,128)(2,1)S(1)} %collective-permute-done.6.refs_8_), channel_id=1, source_target_pairs={{0,28},{4,0},{8,4},{12,8},{16,12},{20,16},{24,20},{28,24},{1,29},{... | collective-permute-start | bytes 2359304 | tf_op jit(solution)/shard_map/ppermute | solution.py:143
  50.3 20.5 %collective-permute-start.2 = (bf16[8,128,384]{2,1,0:T(8,128)(2,1)S(1)}, bf16[8,128,384]{2,1,0:T(8,128)(2,1)S(1)}, u32[]{:S(2)}, u32[]{:S(2)}) collective-permute-start(bf16[8,128,384]{2,1,0:T(8,128)(2,1)S(1)} %get-tuple-element.68), channel_id=1, source_target_pairs={{0,3},{1,2},{2,1},{3,0},{4,7},{5,6},{6,5},{7,4},{8,11},{9,10},{10,... | collective-permute-start | bytes 2359304 | tf_op jit(solution)/shard_map/ppermute | solution.py:202
  63.4 11.4 %collective-permute-start.11 = (bf16[192,1024]{1,0:T(8,128)(2,1)S(1)}, bf16[192,1024]{1,0:T(8,128)(2,1)S(1)}, u32[]{:S(2)}, u32[]{:S(2)}) collective-permute-start(bf16[192,1024]{1,0:T(8,128)(2,1)S(1)} %slice.76), channel_id=1, source_target_pairs={{0,4},{4,8},{8,12},{12,16},{16,20},{20,24},{24,28},{28,0},{1,5},{5... | collective-permute-start | bytes 1179656 | tf_op jit(solution)/shard_map/ppermute | solution.py:143
  76.2 11.7 %collective-permute-start.21 = (f32[1,1,1,64,384]{4,3,2,1,0:T(8,128)S(1)}, f32[1,1,1,64,384]{4,3,2,1,0:T(8,128)S(1)}, u32[]{:S(2)}, u32[]{:S(2)}) collective-permute-start(f32[1,1,1,64,384]{4,3,2,1,0:T(8,128)S(1)} %slice_select_fusion.1), channel_id=1, source_target_pairs={{0,128},{128,0},{1,129},{129,1},{2,130},{130,2},{3,131},{131,3},{4... | collective-permute-start | bytes 294920 | tf_op jit(solution)/shard_map/ppermute | solution.py:189
  78.7 10.7 %collective-permute-start.18 = (bf16[128,512]{1,0:T(8,128)(2,1)S(1)}, bf16[128,512]{1,0:T(8,128)(2,1)S(1)}, u32[]{:S(2)}, u32[]{:S(2)}) collective-permute-start(bf16[128,512]{1,0:T(8,128)(2,1)S(1)} %fusion.17), channel_id=1, source_target_pairs={{0,2},{2,0},{1,3},{3,1},{4,6},{6,4},{5,7},{7,5},{8,10},{10,8},{9,1... | collective-permute-start | bytes 393224 | tf_op jit(solution)/shard_map/ppermute | solution.py:229
  107.1 14.5 %collective-permute-start.27 = (bf16[2,1,1,64,384]{4,3,2,1,0:T(8,128)(2,1)S(1)}, bf16[2,1,1,64,384]{4,3,2,1,0:T(8,128)(2,1)S(1)}, u32[]{:S(2)}, u32[]{:S(2)}) collective-permute-start(bf16[2,1,1,64,384]{4,3,2,1,0:T(8,128)(2,1)S(1)} %pad_maximum_fusion.10), channel_id=1, source_target_pairs={{0,32},{32,0},{64,96},{96,64},{1,33},{33,1},{65,97},{97,65},{2,34}... | collective-permute-start | bytes 294920 | tf_op jit(solution)/shard_map/ppermute | solution.py:193
  118.1 11.7 %collective-permute-start.23 = (bf16[384,512]{1,0:T(8,128)(2,1)S(1)}, bf16[384,512]{1,0:T(8,128)(2,1)S(1)}, u32[]{:S(2)}, u32[]{:S(2)}) collective-permute-start(bf16[384,512]{1,0:T(8,128)(2,1)S(1)} %pad_maximum_fusion.2), channel_id=1, source_target_pairs={{0,4},{4,8},{8,12},{12,16},{16,20},{20,24},{24,28},{28,0},{1,5},{5... | collective-permute-start | bytes 1179656 | tf_op jit(solution)/shard_map/ppermute | solution.py:143
  119.8 10.0 %collective-permute-start.24 = (bf16[384,512]{1,0:T(8,128)(2,1)S(1)}, bf16[384,512]{1,0:T(8,128)(2,1)S(1)}, u32[]{:S(2)}, u32[]{:S(2)}) collective-permute-start(bf16[384,512]{1,0:T(8,128)(2,1)S(1)} %pad_maximum_fusion.3), channel_id=1, source_target_pairs={{0,28},{4,0},{8,4},{12,8},{16,12},{20,16},{24,20},{28,24},{1,29},{... | collective-permute-start | bytes 1179656 | tf_op jit(solution)/shard_map/ppermute | solution.py:143
  129.8 10.0 %collective-permute-start.32 = (bf16[2,1,2,64,384]{4,3,2,1,0:T(8,128)(2,1)S(1)}, bf16[2,1,2,64,384]{4,3,2,1,0:T(8,128)(2,1)S(1)}, u32[]{:S(2)}, u32[]{:S(2)}) collective-permute-start(bf16[2,1,2,64,384]{4,3,2,1,0:T(8,128)(2,1)S(1)} %pad_maximum_fusion.9), channel_id=1, source_target_pairs={{0,64},{32,96},{64,0},{96,32},{1,65},{33,97},{65,1},{97,33},{2,66}... | collective-permute-start | bytes 589832 | tf_op jit(solution)/shard_map/ppermute | solution.py:193
  133.5 17.2 %collective-permute-start.29 = (bf16[384,512]{1,0:T(8,128)(2,1)S(1)}, bf16[384,512]{1,0:T(8,128)(2,1)S(1)}, u32[]{:S(2)}, u32[]{:S(2)}) collective-permute-start(bf16[384,512]{1,0:T(8,128)(2,1)S(1)} %fusion.4), channel_id=1, source_target_pairs={{0,28},{4,0},{8,4},{12,8},{16,12},{20,16},{24,20},{28,24},{1,29},{... | collective-permute-start | bytes 1179656 | tf_op jit(solution)/shard_map/ppermute | solution.py:143
  136.6 14.2 %collective-permute-start.28 = (bf16[384,512]{1,0:T(8,128)(2,1)S(1)}, bf16[384,512]{1,0:T(8,128)(2,1)S(1)}, u32[]{:S(2)}, u32[]{:S(2)}) collective-permute-start(bf16[384,512]{1,0:T(8,128)(2,1)S(1)} %fusion.3), channel_id=1, source_target_pairs={{0,4},{4,8},{8,12},{12,16},{16,20},{20,24},{24,28},{28,0},{1,5},{5... | collective-permute-start | bytes 1179656 | tf_op jit(solution)/shard_map/ppermute | solution.py:143
  136.6 14.1 %collective-permute-start.30 = (bf16[192,512]{1,0:T(8,128)(2,1)S(1)}, bf16[192,512]{1,0:T(8,128)(2,1)S(1)}, u32[]{:S(2)}, u32[]{:S(2)}) collective-permute-start(bf16[192,512]{1,0:T(8,128)(2,1)S(1)} %get-tuple-element.107), channel_id=1, source_target_pairs={{0,4},{4,8},{8,12},{12,16},{16,20},{20,24},{24,28},{28,0},{1,5},{5... | collective-permute-start | bytes 589832 | tf_op jit(solution)/shard_map/ppermute | solution.py:143
  137.0 10.3 %collective-permute-start.31 = (bf16[192,512]{1,0:T(8,128)(2,1)S(1)}, bf16[192,512]{1,0:T(8,128)(2,1)S(1)}, u32[]{:S(2)}, u32[]{:S(2)}) collective-permute-start(bf16[192,512]{1,0:T(8,128)(2,1)S(1)} %get-tuple-element.108), channel_id=1, source_target_pairs={{0,28},{4,0},{8,4},{12,8},{16,12},{20,16},{24,20},{28,24},{1,29},{... | collective-permute-start | bytes 589832 | tf_op jit(solution)/shard_map/ppermute | solution.py:143
  150.8 12.0 %collective-permute-start.36 = (bf16[384,512]{1,0:T(8,128)(2,1)S(1)}, bf16[384,512]{1,0:T(8,128)(2,1)S(1)}, u32[]{:S(2)}, u32[]{:S(2)}) collective-permute-start(bf16[384,512]{1,0:T(8,128)(2,1)S(1)} %pad_maximum_fusion.6), channel_id=1, source_target_pairs={{0,28},{4,0},{8,4},{12,8},{16,12},{20,16},{24,20},{28,24},{1,29},{... | collective-permute-start | bytes 1179656 | tf_op jit(solution)/shard_map/ppermute | solution.py:143
  151.3 13.2 %collective-permute-start.35 = (bf16[384,512]{1,0:T(8,128)(2,1)S(1)}, bf16[384,512]{1,0:T(8,128)(2,1)S(1)}, u32[]{:S(2)}, u32[]{:S(2)}) collective-permute-start(bf16[384,512]{1,0:T(8,128)(2,1)S(1)} %pad_maximum_fusion.5), channel_id=1, source_target_pairs={{0,4},{4,8},{8,12},{12,16},{16,20},{20,24},{24,28},{28,0},{1,5},{5... | collective-permute-start | bytes 1179656 | tf_op jit(solution)/shard_map/ppermute | solution.py:143
  153.7 15.0 %collective-permute-start.33 = (bf16[384,512]{1,0:T(8,128)(2,1)S(1)}, bf16[384,512]{1,0:T(8,128)(2,1)S(1)}, u32[]{:S(2)}, u32[]{:S(2)}) collective-permute-start(bf16[384,512]{1,0:T(8,128)(2,1)S(1)} %fusion.2), channel_id=1, source_target_pairs={{0,4},{4,8},{8,12},{12,16},{16,20},{20,24},{24,28},{28,0},{1,5},{5... | collective-permute-start | bytes 1179656 | tf_op jit(solution)/shard_map/ppermute | solution.py:143
  153.8 14.9 %collective-permute-start.34 = (bf16[384,512]{1,0:T(8,128)(2,1)S(1)}, bf16[384,512]{1,0:T(8,128)(2,1)S(1)}, u32[]{:S(2)}, u32[]{:S(2)}) collective-permute-start(bf16[384,512]{1,0:T(8,128)(2,1)S(1)} %fusion.5), channel_id=1, source_target_pairs={{0,28},{4,0},{8,4},{12,8},{16,12},{20,16},{24,20},{28,24},{1,29},{... | collective-permute-start | bytes 1179656 | tf_op jit(solution)/shard_map/ppermute | solution.py:143
  (23 other events, 192.7 us)
